TPU v7x, 32 devices: a whole 2x2x4 slice. The times are simulated.
32 devices in a mesh: seq: 8 (over z, y), heads: 4 (over x, core).
Axes of the slice: x: 2, y: 2, z: 4, core: 2. Of those that a mesh axis runs over, the one named last changes fastest.
Arguments:
- fwd_tokens: bfloat16 [2048, 4096], P('seq'), may hold values from -6 to 6
- bwd_tokens: bfloat16 [2048, 4096], P('seq'), may hold values from -6 to 6
- qkv_weight: bfloat16 [4096, 3072], P('seq', 'heads'), may hold values from -0.09375 to 0.09375
- head_gain: float32 [1024], P('heads'), may hold values from 0.1 to 1.9
- out_cotangent: float32 [2048, 1024], P('seq', 'heads'), may hold values from -6 to 6
- initial_state: float32 [2, 4, 256, 256], P(None, 'heads'), may hold values from -192 to 192
Outputs:
- fwd_output: float32 [2048, 1024], P('seq', 'heads')
- bwd_token_grad: bfloat16 [2048, 4096], P('seq', 'heads')
All inputs are finite; a program needn't handle non-finite values.
Results may differ from a plain program's by a relative error of at most 0.02.
Values may be sent and summed in bfloat16 or wider, within the bound.
A program may use at most 64 MiB of HBM per device.

v0:
```python
import jax
import jax.numpy as jnp
from jax import lax
from jax.sharding import PartitionSpec as P

highest = lax.Precision.HIGHEST
epsilon = 1e-06


def entering(value, axis, combine, identity):
    peers, place = (lax.axis_size(axis), lax.axis_index(axis))
    everything = jax.tree.map(
        lambda part, kind: lax.all_gather(part.astype(kind), axis),
        value,
        (jnp.bfloat16, jnp.bfloat16),
    )
    start = jax.tree.map(
        lambda part, zero: jnp.broadcast_to(jnp.asarray(zero, part.dtype), part.shape),
        value,
        identity,
    )

    def lap(k, before):
        reached = k < place
        new = combine(
            before, jax.tree.map(lambda part, own: part[k].astype(own.dtype), everything, value)
        )
        return jax.tree.map(lambda a, b: jnp.where(reached, a, b), new, before)

    return lax.fori_loop(0, peers, lap, start)


def entering_2(value, axis, combine, identity):
    peers, place = (lax.axis_size(axis), lax.axis_index(axis))
    everything = lax.all_gather(
        value.astype(jnp.bfloat16 if value.dtype == jnp.float32 else value.dtype), axis
    )
    start = jnp.broadcast_to(jnp.asarray(identity, value.dtype), value.shape)

    def lap(k, before):
        at = peers - 1 - k
        reached = at > place
        new = combine(before, everything[at].astype(value.dtype))
        return jnp.where(reached, new, before)

    return lax.fori_loop(0, peers, lap, start)


def add_pair(earlier, later):
    return (earlier[0] + later[0], earlier[1] + later[1])


def add_single(earlier, later):
    return earlier + later


def block_forward(queries, keys, values, prefix, causal):
    scores = jnp.dot(queries, keys.T, precision=highest) * causal
    output = jnp.dot(queries, prefix, precision=highest) + jnp.dot(
        scores, values, precision=highest
    )
    return (output, scores)


def body(fwd_tokens, bwd_tokens, qkv_weight, head_gain, out_cotangent, initial_state):
    width = head_gain.shape[0]
    rows = fwd_tokens.shape[0]
    whole = lax.all_gather(qkv_weight, "seq", axis=0, tiled=True)
    proj_fwd = jnp.dot(fwd_tokens, whole, preferred_element_type=jnp.float32)
    proj_bwd = jnp.dot(bwd_tokens, whole, preferred_element_type=jnp.float32)
    positions = lax.broadcasted_iota(jnp.int32, (rows, rows), 0)
    others = lax.broadcasted_iota(jnp.int32, (rows, rows), 1)
    causal = (others <= positions).astype(jnp.float32)
    queries_f, keys_f, values_f = (
        proj_fwd[:, :width],
        proj_fwd[:, width : 2 * width],
        proj_fwd[:, 2 * width :],
    )
    queries, keys, values = (
        proj_bwd[:, :width],
        proj_bwd[:, width : 2 * width],
        proj_bwd[:, 2 * width :],
    )
    state_fwd = jnp.dot(keys_f.T, values_f, precision=highest)
    state_bwd = jnp.dot(keys.T, values, precision=highest)
    zero_state = jnp.zeros((width, width), jnp.float32)
    prefix_fwd, prefix = entering((state_fwd, state_bwd), "seq", add_pair, (zero_state, zero_state))
    prefix_fwd = prefix_fwd + initial_state[0, 0]
    prefix = prefix + initial_state[1, 0]
    output, scores = block_forward(queries, keys, values, prefix, causal)
    scale = lax.rsqrt(jnp.mean(output * output, -1, keepdims=True) + epsilon)
    weighted = out_cotangent * head_gain
    d_out = scale * weighted - output * scale**3 * jnp.mean(output * weighted, -1, keepdims=True)
    d_state = jnp.dot(queries.T, d_out, precision=highest)
    suffix = entering_2(d_state, "seq", add_single, zero_state)
    out_fwd, scores_fwd = block_forward(queries_f, keys_f, values_f, prefix_fwd, causal)
    scale_fwd = lax.rsqrt(jnp.mean(out_fwd * out_fwd, -1, keepdims=True) + epsilon)
    fwd_output = out_fwd * scale_fwd * head_gain
    d_scores = jnp.dot(d_out, values.T, precision=highest) * causal
    d_query = jnp.dot(d_out, prefix.T, precision=highest) + jnp.dot(
        d_scores, keys, precision=highest
    )
    d_key = jnp.dot(values, suffix.T, precision=highest) + jnp.dot(
        d_scores.T, queries, precision=highest
    )
    d_value = jnp.dot(keys, suffix, precision=highest) + jnp.dot(scores.T, d_out, precision=highest)
    d_proj = jnp.concatenate([d_query, d_key, d_value], 1).astype(jnp.bfloat16)
    dims = (((1,), (1,)), ((), ()))
    grad_t = lax.psum_scatter(
        lax.dot_general(whole, d_proj, dims, preferred_element_type=jnp.float32).astype(
            jnp.bfloat16
        ),
        "heads",
        scatter_dimension=0,
        tiled=True,
    ).astype(jnp.float32)
    return (fwd_output, grad_t.T.astype(jnp.bfloat16))


def solution(mesh):
    return jax.shard_map(
        body,
        mesh=mesh,
        in_specs=(
            P("seq", None),
            P("seq", None),
            P("seq", "heads"),
            P("heads"),
            P("seq", "heads"),
            P(None, "heads", None, None),
        ),
        out_specs=(P("seq", "heads"), P("seq", "heads")),
        check_vma=False,
    )
```

profile of v0, /device:TPU:0, one launch (start us, length us, event | category | flops | bytes accessed | tf_op | source)
XLA Modules:
  0.0 310.6 jit_solution(1446474593609692167)
XLA Ops:
  8.0 104.0 %all-gather.8.cloned.1.call-done = bf16[4096,768]{1,0:T(8,128)(2,1)} async-done(((bf16[512,768]{1,0:T(8,128)(2,1)}), bf16[4096,768]{1,0:T(8,128)(2,1)}) %all-gather.8.cloned.1.call-update) | async-done | bytes 6291472 | tf_op jit(solution)/shard_map/all_gather | solution.py:68
  112.0 4.6 %fusion.35 = f32[256,768]{1,0:T(8,128)S(1)} fusion(bf16[256,4096]{1,0:T(8,128)(2,1)S(1)} %copy-done, bf16[4096,768]{1,0:T(8,128)(2,1)} %all-gather.8.cloned.1.call-done), kind=kOutput, calls=%fused_computation.62 | convolution fusion | flops 1610612736 | bytes 9175040 | tf_op jit(solution)/shard_map/dot_general | solution.py:70
  116.5 1.2 convolution_convert_fusion.2
  117.9 5.2 %fusion.34 = f32[256,768]{1,0:T(8,128)S(1)} fusion(bf16[256,4096]{1,0:T(8,128)(2,1)} %param.10, bf16[4096,768]{1,0:T(8,128)(2,1)} %all-gather.8.cloned.1.call-done), kind=kOutput, calls=%fused_computation.61 | convolution fusion | flops 1610612736 | bytes 9175040 | tf_op jit(solution)/shard_map/dot_general | solution.py:69
  124.0 1.2 convolution_convert_fusion.3
  125.4 1.8 copy.8
  127.2 1.1 convolution_select_fusion.1
  128.3 2.1 convolution_select_fusion.2
  130.4 25.9 %all-gather.12.cloned.1.call-done = bf16[2048,256]{1,0:T(8,128)(2,1)} async-done(((bf16[256,256]{1,0:T(8,128)(2,1)}), bf16[2048,256]{1,0:T(8,128)(2,1)}) %all-gather.12.cloned.1.call-update) | async-done | bytes 1048592 | tf_op jit(solution)/shard_map/all_gather | solution.py:13
  156.4 41.1 %all-gather.10.cloned.1.call-done = bf16[2048,256]{1,0:T(8,128)(2,1)} async-done(((bf16[256,256]{1,0:T(8,128)(2,1)}), bf16[2048,256]{1,0:T(8,128)(2,1)}) %all-gather.10.cloned.1.call-update) | async-done | bytes 1048592 | tf_op jit(solution)/shard_map/all_gather | solution.py:13
  197.4 9.4 %while.32 = (s32[]{:T(128)}, f32[256,256]{1,0:T(8,128)S(1)}, f32[256,256]{1,0:T(8,128)S(1)}, s32[]{:T(128)}, bf16[8,256,256]{2,1,0:T(8,128)(2,1)}, /*index=5*/bf16[8,256,256]{2,1,0:T(8,128)(2,1)}, s32[]{:T(128)}, s32[]{:T(128)}) while((s32[]{:T(128)}, f32[256,256]{1,0:T(8,128)S(1)}, f32[256,256]{1,0:T(8,128)S(1)}, s32[]{:T(128)}, ...), condition=%wide.region_1.2_spmd.clone, body=%wide.region_0.1_spmd.clone.sunk | while | flops 524292 | bytes 1310829 | solution.py:30
  197.4 1.2 add_select_fusion.5
  198.6 1.2 add_select_fusion.5
  199.8 1.2 add_select_fusion.5
  201.0 1.2 add_select_fusion.5
  202.1 1.2 add_select_fusion.5
  203.3 1.2 add_select_fusion.5
  204.5 1.2 add_select_fusion.5
  205.7 1.2 add_select_fusion.5
  206.9 1.6 fusion.20
  208.4 1.6 fusion.9
  210.1 1.6 multiply_reduce_fusion.2
  211.7 1.6 multiply_reduce_fusion.1
  214.9 1.3 convolution_convert_fusion.1
  216.5 1.5 convolution_select_fusion
  218.0 1.7 fusion.32
  220.1 35.1 %all-gather.14.cloned.1.call-done = bf16[2048,256]{1,0:T(8,128)(2,1)} async-done(((bf16[256,256]{1,0:T(8,128)(2,1)}), bf16[2048,256]{1,0:T(8,128)(2,1)}) %all-gather.14.cloned.1.call-update) | async-done | bytes 1048592 | tf_op jit(solution)/shard_map/all_gather | solution.py:35
  255.3 8.5 %while.33 = (s32[]{:T(128)}, f32[256,256]{1,0:T(8,128)S(1)}, s32[]{:T(128)}, bf16[8,256,256]{2,1,0:T(8,128)(2,1)}, s32[]{:T(128)}, /*index=5*/s32[]{:T(128)}, s32[]{:T(128)}, s32[]{:T(128)}) while((s32[]{:T(128)}, f32[256,256]{1,0:T(8,128)S(1)}, s32[]{:T(128)}, bf16[8,256,256]{2,1,0:T(8,128)(2,1)}, s32[]{:T(128)}, ...), condition=%wide.region_6.7_spmd.clone, body=%wide.region_5.6_spmd.clone.sunk | while | flops 262152 | bytes 655515 | solution.py:46
  264.5 1.5 fusion.2
  266.1 1.5 fusion.3
  267.7 6.0 %fusion = bf16[4096,256]{0,1:T(8,128)(2,1)} fusion(bf16[4096,768]{1,0:T(8,128)(2,1)} %all-gather.8.cloned.1.call-done, bf16[256,256]{1,0:T(8,128)(2,1)S(1)} %fusion.3, bf16[256,256]{1,0:T(8,128)(2,1)S(1)} %fusion.2, bf16[256,256]{1,0:T(8,128)(2,1)S(1)} %fusion.1), kind=kOutput, calls=%fused_computation.4 | convolution fusion | flops 1612840960 | bytes 8781824 | tf_op jit(solution)/shard_map/dot_general | solution.py:110
  274.6 29.5 %reduce-scatter.2.cloned.1.call-done = bf16[1024,256]{0,1:T(8,128)(2,1)} async-done(((bf16[4096,256]{0,1:T(8,128)(2,1)}), bf16[1024,256]{0,1:T(8,128)(2,1)}) %reduce-scatter.2.cloned.1.call-update) | async-done | bytes 524304 | tf_op jit(solution)/shard_map/reduce_scatter | solution.py:109
  (44 shorter events, 13.9 us)
Async XLA Ops:
  7.2 104.8 %copy-start = (bf16[256,4096]{1,0:T(8,128)(2,1)S(1)}, bf16[256,4096]{1,0:T(8,128)(2,1)}, u32[]{:S(2)}) copy-start(bf16[256,4096]{1,0:T(8,128)(2,1)} %param.11) | copy-start | bytes 6291460
  7.2 104.8 %all-gather.8.cloned.1.call-start = ((), (), s32[]{:S(2)}) async-start(), calls=%async_computation.1 | async-start | bytes 7077888 | tf_op jit(solution)/shard_map/all_gather | solution.py:68
  7.9 148.4 %all-gather.12.cloned.1.call-start = ((), (), s32[]{:S(2)}) async-start(), calls=%async_computation.4 | async-start | bytes 1179648 | tf_op jit(solution)/shard_map/all_gather | solution.py:13
  117.8 79.6 %all-gather.10.cloned.1.call-start = ((), (), s32[]{:S(2)}) async-start(), calls=%async_computation.3 | async-start | bytes 1179648 | tf_op jit(solution)/shard_map/all_gather | solution.py:13
  123.1 1.0 copy-start.3
  125.3 130.0 %all-gather.14.cloned.1.call-start = ((), (), s32[]{:S(2)}) async-start(), calls=%async_computation.5 | async-start | bytes 1179648 | tf_op jit(solution)/shard_map/all_gather | solution.py:35
  197.4 14.3 %copy-start.7 = (f32[256]{0:T(256)S(1)}, f32[256]{0:T(256)}, u32[]{:S(2)}) copy-start(f32[256]{0:T(256)} %param.13) | copy-start | bytes 3076
  206.8 6.6 %copy-start.5 = (f32[256,256]{0,1:T(8,128)S(1)}, f32[256,256]{0,1:T(8,128)}, u32[]{:S(2)}) copy-start(f32[256,256]{0,1:T(8,128)} %copy.8) | copy-start | bytes 786436
  214.2 0.7 copy-start.1
  216.2 87.8 %reduce-scatter.2.cloned.1.call-start = ((), (), s32[]{:S(2)}) async-start(), calls=%async_computation.2 | async-start | bytes 2621440 | tf_op jit(solution)/shard_map/reduce_scatter | solution.py:109
  218.0 1.7 copy-start.4
  219.7 46.4 %copy-start.2 = (f32[256,256]{0,1:T(8,128)S(1)}, f32[256,256]{0,1:T(8,128)}, u32[]{:S(2)}) copy-start(f32[256,256]{0,1:T(8,128)} %copy-done.1) | copy-start | bytes 786436
  267.7 6.1 %copy-start.6 = (f32[256,256]{0,1:T(8,128)S(1)}, f32[256,256]{0,1:T(8,128)}, u32[]{:S(2)}) copy-start(f32[256,256]{0,1:T(8,128)} %get-tuple-element.288) | copy-start | bytes 786436
Sparse Core Ops, SparseCore 0:
  10.2 101.7 all-gather.7
  117.9 38.3 all-gather.11
  158.5 38.8 all-gather.9
  216.3 38.8 all-gather.13
  273.8 30.1 reduce-scatter.1
where the time goes:
time: 311 us
  waiting for transfers between devices  236 us (76%)
  matrix products  36.8 us (12%)
  other arithmetic  18.3 us (6%)
  between operations  14 us (5%)
  local copies, waits for them, and re-layouts  4.32 us (1%)
    all_gather x1, waiting for transfers between devices, body(): whole = lax.all_gather(qkv_weight, 'seq', axis=0, tiled=True)  104 us
    all_gather x2, waiting for transfers between devices, entering(): lax.all_gather(part.astype(kind), axis)  67 us
    all_gather x1, waiting for transfers between devices, entering_2(): lax.all_gather(value.astype(jnp.bfloat16 if value.dtype == jnp.float32 el...  35.1 us
    reduce_scatter x1, waiting for transfers between devices, body(): lax.psum_scatter(lax.dot_general(whole, d_proj, dims, preferred_element_t...  29.5 us
    select_n x8, other arithmetic, lap(): return jax.tree.map(lambda a, b: jnp.where(reached, a, b), new, before)  9.24 us
    select_n x8, other arithmetic, lap(): return jnp.where(reached, new, before)  8.26 us
  transfers between devices with their start and end apart: 5, of which 5 were waited for; matrix products, arithmetic and copies ran while one was open for 5% of the time, Pallas kernels for 0%

commit v1 on v0

v1 whole, which is shorter than its diff:
```python
import functools

import jax
import jax.numpy as jnp
from jax import lax
from jax.experimental import pallas as pl
from jax.experimental.pallas import tpu as pltpu
from jax.sharding import PartitionSpec as P

MESH = pl.DeviceIdType.MESH
BF16 = jnp.bfloat16
F32 = jnp.float32
epsilon = 1e-06


def dot(a, b):
    return lax.dot_general(a, b, (((1,), (0,)), ((), ())), preferred_element_type=F32)


def dot_t(a, b):
    return lax.dot_general(a, b, (((1,), (1,)), ((), ())), preferred_element_type=F32)


def t_dot(a, b):
    return lax.dot_general(a, b, (((0,), (0,)), ((), ())), preferred_element_type=F32)


def kernel(
    n,
    hn,
    xf_ref,
    xb_ref,
    w_ref,
    gain_ref,
    cot_ref,
    init_ref,
    of_ref,
    ob_ref,
    xbuf,
    wbuf,
    acc,
    cot,
    init,
    st_own,
    st_peer,
    st_tot,
    st_z,
    st_half,
    st_far,
    half32,
    whole32,
    c_send,
    c_recv,
    x_send,
    x_recv,
    load_sem,
    wsend,
    wrecv,
    st_ssem,
    st_rsem,
    z_ssem,
    z_rsem,
    c_ssem,
    c_rsem,
    x_ssem,
    x_rsem,
):
    s, h = lax.axis_index("seq"), lax.axis_index("heads")
    chain, pairs = n // 2, hn // 2
    a, b = lax.div(s, 2), lax.rem(s, 2)
    xh, c = lax.div(h, 2), lax.rem(h, 2)
    mate = a * 2 + 1 - b
    twin = xh * 2 + 1 - c
    tokens = xf_ref.shape[0]
    depth = w_ref.shape[0]
    width = gain_ref.shape[1]
    half = width // 2
    feat = ob_ref.shape[1]

    def rows_of(source):
        return pl.ds(pl.multiple_of(source * depth, depth), depth)

    w_loads = [
        pltpu.make_async_copy(
            w_ref.at[:, pl.ds(p * width, width)], wbuf.at[p, rows_of(s)], load_sem.at[p]
        )
        for p in range(3)
    ]
    x_loads = [
        pltpu.make_async_copy(xf_ref, xbuf.at[pl.ds(0, tokens)], load_sem.at[3]),
        pltpu.make_async_copy(xb_ref, xbuf.at[pl.ds(tokens, tokens)], load_sem.at[4]),
    ]
    o_loads = [
        pltpu.make_async_copy(cot_ref, cot, load_sem.at[5]),
        pltpu.make_async_copy(init_ref, init, load_sem.at[6]),
    ]
    for p in (1, 2, 0):
        w_loads[p].start()
    for load in x_loads + o_loads:
        load.start()

    barrier = pltpu.get_barrier_semaphore()

    def greet(seq_index, head_index):
        pl.semaphore_signal(barrier, inc=1, device_id=(seq_index, head_index), device_id_type=MESH)

    for e in range(1, chain):
        greet(lax.rem(a + e, chain) * 2 + b, h)
    greet(mate, h)
    for e in range(1, pairs):
        greet(s, lax.rem(xh + e, pairs) * 2 + c)
    greet(s, twin)
    pl.semaphore_wait(barrier, chain + pairs)

    UP, DOWN, CROSS = 0, 1, 2

    def shard_copy(p, sa, sb, way):
        source = sa * 2 + sb
        to = {UP: s + 2, DOWN: s - 2, CROSS: mate}[way]
        return pltpu.make_async_remote_copy(
            src_ref=wbuf.at[p, rows_of(source)],
            dst_ref=wbuf.at[p, rows_of(source)],
            send_sem=wsend.at[way, sa, p],
            recv_sem=wrecv.at[source, p],
            device_id=(to, h),
            device_id_type=MESH,
        )

    def project(source, pieces):
        x = xbuf[:, pl.ds(pl.multiple_of(source * depth, depth), depth)]
        for p in pieces:
            acc[p] += dot(x, wbuf[p, rows_of(source)])

    def start_up(p, sa):
        @pl.when(a < chain - 1)
        def _():
            shard_copy(p, sa, b, UP).start()

    def start_down(p, sa):
        @pl.when(a > 0)
        def _():
            shard_copy(p, sa, b, DOWN).start()

    def arrivals(d, pieces, then_own):
        @pl.when(a - d >= 0)
        def _():
            for p in pieces:
                shard_copy(p, a - d, b, CROSS).wait_recv()
                start_up(p, a - d)
                shard_copy(p, a - d, b, CROSS).start()

            @pl.when(a - d == 0)
            def _():
                for p in then_own:
                    start_up(p, a)

        @pl.when(a + d < chain)
        def _():
            for p in pieces:
                shard_copy(p, a + d, b, CROSS).wait_recv()
                start_down(p, a + d)
                shard_copy(p, a + d, b, CROSS).start()

            @pl.when(a + d == chain - 1)
            def _():
                for p in then_own:
                    start_down(p, a)

        @pl.when(a - d >= 0)
        def _():
            project((a - d) * 2 + b, pieces)

        @pl.when(a + d < chain)
        def _():
            project((a + d) * 2 + b, pieces)

    def crossed(sa, pieces):
        for p in pieces:
            shard_copy(p, sa, 1 - b, CROSS).wait_recv()
        project(sa * 2 + 1 - b, pieces)

    def crossings(d, pieces):
        @pl.when(a - d >= 0)
        def _():
            crossed(a - d, pieces)

        @pl.when((a + d < chain) & (d > 0))
        def _():
            crossed(a + d, pieces)

    kv, q_only = (1, 2), (0,)
    for p in kv:
        w_loads[p].wait()
        start_up(p, a)
        start_down(p, a)
        shard_copy(p, a, b, CROSS).start()
    w_loads[0].wait()

    @pl.when(a == 0)
    def _():
        start_up(0, a)

    @pl.when(a == chain - 1)
    def _():
        start_down(0, a)

    acc[...] = jnp.zeros_like(acc)
    for load in x_loads:
        load.wait()
    project(s, (0, 1, 2))

    def kv_lap(d, carry):
        arrivals(d, kv, q_only)
        crossings(d - 1, kv)
        return carry

    lax.fori_loop(1, chain, kv_lap, 0)
    shard_copy(0, a, b, CROSS).start()
    crossings(chain - 1, kv)

    my_half = pl.ds(pl.multiple_of(b * half, half), half)
    far_half = pl.ds(pl.multiple_of((1 - b) * half, half), half)

    def step1_copy(i):
        return pltpu.make_async_remote_copy(
            src_ref=st_own.at[i],
            dst_ref=st_peer.at[i],
            send_sem=st_ssem.at[i, 0],
            recv_sem=st_rsem.at[i, 0],
            device_id=(mate, h),
            device_id_type=MESH,
        )

    def step2_copy(i, to, slot):
        return pltpu.make_async_remote_copy(
            src_ref=st_tot.at[i],
            dst_ref=st_z.at[i, slot],
            send_sem=z_ssem.at[i, to],
            recv_sem=z_rsem.at[i, slot],
            device_id=(to * 2 + b, h),
            device_id_type=MESH,
        )

    def step3_copy(i):
        return pltpu.make_async_remote_copy(
            src_ref=st_half.at[i],
            dst_ref=st_far.at[i],
            send_sem=st_ssem.at[i, 1],
            recv_sem=st_rsem.at[i, 1],
            device_id=(mate, h),
            device_id_type=MESH,
        )

    def after(i, x, y):
        return (x < y) if i == 2 else (x > y)

    def takes(i):
        return (a < chain - 1) if i == 2 else (a > 0)

    def step1(i, state):
        st_own[i] = state.astype(BF16)
        step1_copy(i).start()

    def step2(i):
        step1_copy(i).wait_recv()
        st_tot[i] = (st_own[i, my_half].astype(F32) + st_peer[i, my_half].astype(F32)).astype(BF16)
        for e in range(1, chain):
            for to in (a - e, a + e):

                @pl.when(after(i, to, a) & (to >= 0) & (to < chain))
                def _():
                    step2_copy(i, to, a).start()

    def step3(i):
        half32[...] = jnp.zeros_like(half32)
        for source in range(chain):

            @pl.when(after(i, a, source))
            def _():
                step2_copy(i, source, source).wait_recv()
                half32[...] += st_z[i, source].astype(F32)

        st_half[i] = half32[...].astype(BF16)

        @pl.when(takes(i))
        def _():
            step3_copy(i).start()

        @pl.when(jnp.logical_not(takes(i)))
        def _():
            st_far[i] = jnp.zeros_like(st_far[i])

    def step4(i):
        @pl.when(takes(i))
        def _():
            step3_copy(i).wait_recv()

        whole32[my_half] = st_half[i].astype(F32)
        whole32[far_half] = st_far[i].astype(F32)

        @pl.when(b == (0 if i == 2 else 1))
        def _():
            whole32[...] += st_peer[i].astype(F32)

        return whole32[...]

    def part(p, mb):
        return acc[p, pl.ds(mb * tokens, tokens)].astype(BF16)

    kb, vb = part(1, 1), part(2, 1)
    step1(0, t_dot(kb, vb))
    step1(1, t_dot(part(1, 0), part(2, 0)))

    def q_lap(d, carry):
        arrivals(d, q_only, ())
        crossings(d - 1, q_only)
        return carry

    lax.fori_loop(1, 2, q_lap, 0)
    step2(0)
    step2(1)
    lax.fori_loop(2, chain, q_lap, 0)
    step3(0)
    step3(1)
    crossings(chain - 1, q_only)

    for load in o_loads:
        load.wait()
    positions = lax.broadcasted_iota(jnp.int32, (tokens, tokens), 0)
    others = lax.broadcasted_iota(jnp.int32, (tokens, tokens), 1)
    causal = others <= positions

    def masked(scores):
        return jnp.where(causal, scores, 0.0).astype(BF16)

    gain = gain_ref[...]
    kb, vb, qb = part(1, 1), part(2, 1), part(0, 1)
    scores = masked(dot_t(qb, kb))
    prefix = (step4(0) + init[1, 0]).astype(BF16)
    output = dot(qb, prefix) + dot(scores, vb)
    scale = lax.rsqrt(jnp.mean(output * output, -1, keepdims=True) + epsilon)
    weighted = cot[...] * gain
    d_out = scale * weighted - output * (
        scale * scale * scale * jnp.mean(output * weighted, -1, keepdims=True)
    )
    d_out = d_out.astype(BF16)
    step1(2, t_dot(qb, d_out))
    d_scores = masked(dot_t(d_out, vb))
    dq = (dot_t(d_out, prefix) + dot(d_scores, kb)).astype(BF16)
    step2(2)
    dk_near = t_dot(d_scores, qb)
    dv_near = t_dot(scores, d_out)

    kf, vf, qf = part(1, 0), part(2, 0), part(0, 0)
    prefix_f = (step4(1) + init[0, 0]).astype(BF16)
    out_f = dot(qf, prefix_f) + dot(masked(dot_t(qf, kf)), vf)
    scale_f = lax.rsqrt(jnp.mean(out_f * out_f, -1, keepdims=True) + epsilon)
    of_ref[...] = out_f * scale_f * gain

    step3(2)
    suffix = step4(2).astype(BF16)
    dk = (dot_t(vb, suffix) + dk_near).astype(BF16)
    dv = (dot(kb, suffix) + dv_near).astype(BF16)

    def piece(j):
        rows = pl.ds(pl.multiple_of(j * feat, feat), feat)
        return dot_t(dq, wbuf[0, rows]) + dot_t(dk, wbuf[1, rows]) + dot_t(dv, wbuf[2, rows])

    def twin_copy(slot):
        return pltpu.make_async_remote_copy(
            src_ref=c_send.at[slot],
            dst_ref=c_recv.at[slot],
            send_sem=c_ssem.at[slot],
            recv_sem=c_rsem.at[slot],
            device_id=(s, twin),
            device_id_type=MESH,
        )

    def pair_copy(to, slot):
        return pltpu.make_async_remote_copy(
            src_ref=x_send.at[to],
            dst_ref=x_recv.at[slot],
            send_sem=x_ssem.at[to],
            recv_sem=x_rsem.at[slot],
            device_id=(s, to * 2 + c),
            device_id_type=MESH,
        )

    def twin_sum(to):
        c_send[to] = piece(to * 2 + 1 - c).astype(BF16)
        twin_copy(to).start()
        mine = piece(to * 2 + c)
        twin_copy(to).wait_recv()
        return mine + c_recv[to].astype(F32)

    def pair_lap(e, carry):
        to = lax.rem(xh + e, pairs)
        x_send[to] = twin_sum(to).astype(BF16)
        pair_copy(to, xh).start()
        return carry

    lax.fori_loop(1, pairs, pair_lap, 0)
    total = twin_sum(xh)
    for e in range(1, pairs):
        source = lax.rem(xh + e, pairs)
        pair_copy(source, source).wait_recv()
        total += x_recv[source].astype(F32)
    ob_ref[...] = total.astype(BF16)

    def drain_chain(sa, carry):
        for p in range(3):
            shard_copy(p, sa, b, CROSS).wait_send()

            @pl.when((sa <= a) & (a < chain - 1))
            def _():
                shard_copy(p, sa, b, UP).wait_send()

            @pl.when((sa >= a) & (a > 0))
            def _():
                shard_copy(p, sa, b, DOWN).wait_send()

        for i in range(3):

            @pl.when(after(i, sa, a))
            def _():
                step2_copy(i, sa, a).wait_send()

        return carry

    lax.fori_loop(0, chain, drain_chain, 0)
    for i in range(3):
        step1_copy(i).wait_send()

        @pl.when(takes(i))
        def _():
            step3_copy(i).wait_send()

    for slot in range(pairs):
        twin_copy(slot).wait_send()
    for e in range(1, pairs):
        pair_copy(lax.rem(xh + e, pairs), xh).wait_send()


def body(n, hn, fwd_tokens, bwd_tokens, qkv_weight, head_gain, out_cotangent, initial_state):
    tokens, model = fwd_tokens.shape
    width = head_gain.shape[0]
    feat = model // hn
    chain, pairs = n // 2, hn // 2
    anywhere = pl.BlockSpec(memory_space=pl.ANY)
    vmem = pl.BlockSpec(memory_space=pltpu.VMEM)
    dma = pltpu.SemaphoreType.DMA
    return pl.pallas_call(
        functools.partial(kernel, n, hn),
        out_shape=(
            jax.ShapeDtypeStruct((tokens, width), F32),
            jax.ShapeDtypeStruct((tokens, feat), BF16),
        ),
        in_specs=[anywhere, anywhere, anywhere, vmem, anywhere, anywhere],
        out_specs=(vmem, vmem),
        scratch_shapes=[
            pltpu.VMEM((2 * tokens, model), BF16),
            pltpu.VMEM((3, model, width), BF16),
            pltpu.VMEM((3, 2 * tokens, width), F32),
            pltpu.VMEM((tokens, width), F32),
            pltpu.VMEM((2, 1, width, width), F32),
            pltpu.VMEM((3, width, width), BF16),
            pltpu.VMEM((3, width, width), BF16),
            pltpu.VMEM((3, width // 2, width), BF16),
            pltpu.VMEM((3, chain, width // 2, width), BF16),
            pltpu.VMEM((3, width // 2, width), BF16),
            pltpu.VMEM((3, width // 2, width), BF16),
            pltpu.VMEM((width // 2, width), F32),
            pltpu.VMEM((width, width), F32),
            pltpu.VMEM((pairs, tokens, feat), BF16),
            pltpu.VMEM((pairs, tokens, feat), BF16),
            pltpu.VMEM((pairs, tokens, feat), BF16),
            pltpu.VMEM((pairs, tokens, feat), BF16),
            dma((7,)),
            dma((3, chain, 3)),
            dma((n, 3)),
            dma((3, 2)),
            dma((3, 2)),
            dma((3, chain)),
            dma((3, chain)),
            dma((pairs,)),
            dma((pairs,)),
            dma((pairs,)),
            dma((pairs,)),
        ],
        compiler_params=pltpu.CompilerParams(
            collective_id=0, has_side_effects=True, vmem_limit_bytes=48 * 1024 * 1024
        ),
    )(fwd_tokens, bwd_tokens, qkv_weight, head_gain.reshape(1, width), out_cotangent, initial_state)


def solution(mesh):
    return jax.shard_map(
        functools.partial(body, mesh.shape["seq"], mesh.shape["heads"]),
        mesh=mesh,
        in_specs=(
            P("seq", None),
            P("seq", None),
            P("seq", "heads"),
            P("heads"),
            P("seq", "heads"),
            P(None, "heads", None, None),
        ),
        out_specs=(P("seq", "heads"), P("seq", "heads")),
        check_vma=False,
    )
```

time: 311 us -> 125 us (0.40)
  waiting for transfers between devices: 236 us -> 0 us
  Pallas kernels: 0 us -> 117 us
  matrix products: 36.8 us -> 0 us
  other arithmetic: 18.3 us -> 0 us
  between operations: 14 us -> 0.65 us
    all_gather x4 -> x0, waiting for transfers between devices: 206 us -> none  [the longest x1 104 us: body(): whole = lax.all_gather(qkv_weight, 'seq', axis=0, tiled=True)]
    pallas_call x0 -> x1, Pallas kernels: none -> 117 us  [body(): pl.pallas_call(functools.partial(kernel, n, hn), out_shape=(jax.ShapeDtyp...]
    dot_general x19 -> x0, matrix products: 36.8 us -> none  [the longest x1 6.02 us: body(): lax.dot_general(whole, d_proj, dims, preferred_element_type=jnp.float32)]
    reduce_scatter x1 -> x0, waiting for transfers between devices: 29.5 us -> none  [body(): lax.psum_scatter(lax.dot_general(whole, d_proj, dims, preferred_element_t...]
    select_n x16 -> x0, other arithmetic: 17.5 us -> none  [the longest x8 9.24 us: lap(): return jax.tree.map(lambda a, b: jnp.where(reached, a, b), new, before)]
    unnamed x18 -> x12, local copies, waits for them, and re-layouts: 4.32 us -> 6.88 us
  transfers between devices with their start and end apart: 5 -> 0, of which waited for: 5 -> 0; matrix products, arithmetic and copies ran while one was open for 5% -> 0% of each run, Pallas kernels for 0% -> 0%
where the time goes in v1:
time: 125 us
  Pallas kernels  117 us (94%)
  local copies, waits for them, and re-layouts  6.88 us (6%)
    pallas_call x1, Pallas kernels, body(): pl.pallas_call(functools.partial(kernel, n, hn), out_shape=(jax.ShapeDtyp...  117 us
    unnamed x12, local copies, waits for them, and re-layouts  6.88 us

profile of v1, /device:TPU:0, one launch (start us, length us, event | category | flops | bytes accessed | tf_op | source)
XLA Modules:
  0.0 124.6 jit_solution(5419725975331113459)
XLA Ops:
  0.6 0.0 copy-start
  0.6 1.6 %copy-done = bf16[256,4096]{1,0:T(8,128)(2,1)S(1)} copy-done((bf16[256,4096]{1,0:T(8,128)(2,1)S(1)}, bf16[256,4096]{1,0:T(8,128)(2,1)}, u32[]{:S(2)}) %copy-start) | copy-done | bytes 2097176
  2.2 0.0 copy-start.1
  2.2 1.1 copy-done.1
  3.4 0.0 copy-start.2
  3.4 1.0 copy-done.2
  4.4 0.0 copy-start.3
  4.4 0.9 copy-done.3
  5.3 0.0 copy-start.4
  5.4 0.7 copy-done.4
  6.0 117.1 %shard_map.77 = (f32[256,256]{1,0:T(8,128)S(1)}, bf16[256,1024]{1,0:T(8,128)(2,1)S(1)}) custom-call(bf16[256,4096]{1,0:T(8,128)(2,1)S(1)} %copy-done, bf16[256,4096]{1,0:T(8,128)(2,1)} %xb_ref.1, bf16[512,768]{1,0:T(8,128)(2,1)S(1)} %copy-done.1, f32[1,256]{1,0:T(1,128)S(1)} %bitcast.1, f32[256,256]{1,0:T(8,128)S(1)} %copy-done.3, ...), custom_call_target="tpu_custom_call" | custom-call | tf_op jit(solution)/shard_map/pallas_call | solution.py:452
  123.1 0.7 copy.10
  123.8 0.8 copy.11
Async XLA Ops:
  0.6 1.6 %copy-start = (bf16[256,4096]{1,0:T(8,128)(2,1)S(1)}, bf16[256,4096]{1,0:T(8,128)(2,1)}, u32[]{:S(2)}) copy-start(bf16[256,4096]{1,0:T(8,128)(2,1)} %xf_ref.1) | copy-start | bytes 6291460
  2.2 1.1 copy-start.1
  3.4 1.0 copy-start.2
  4.4 0.9 copy-start.3
  5.3 0.7 copy-start.4

commit v2 on v1

v2 whole, which is shorter than its diff:
```python
import functools

import jax
import jax.numpy as jnp
from jax import lax
from jax.experimental import pallas as pl
from jax.experimental.pallas import tpu as pltpu
from jax.sharding import PartitionSpec as P

MESH = pl.DeviceIdType.MESH
BF16 = jnp.bfloat16
F32 = jnp.float32
epsilon = 1e-06


def dot(a, b):
    return lax.dot_general(a, b, (((1,), (0,)), ((), ())), preferred_element_type=F32)


def dot_t(a, b):
    return lax.dot_general(a, b, (((1,), (1,)), ((), ())), preferred_element_type=F32)


def t_dot(a, b):
    return lax.dot_general(a, b, (((0,), (0,)), ((), ())), preferred_element_type=F32)


def kernel(
    n,
    hn,
    xf_ref,
    xb_ref,
    w_ref,
    gain_ref,
    cot_ref,
    init_ref,
    of_ref,
    ob_ref,
    xbuf,
    wbuf,
    acc,
    cot,
    init,
    gain,
    st_own,
    st_peer,
    st_tot,
    st_z,
    st_half,
    st_far,
    half32,
    whole32,
    c_send,
    c_recv,
    x_send,
    x_recv,
    load_sem,
    wsend,
    wrecv,
    st_ssem,
    st_rsem,
    z_ssem,
    z_rsem,
    c_ssem,
    c_rsem,
    x_ssem,
    x_rsem,
):
    s, h = lax.axis_index("seq"), lax.axis_index("heads")
    chain, pairs = n // 2, hn // 2
    a, b = lax.div(s, 2), lax.rem(s, 2)
    xh, c = lax.div(h, 2), lax.rem(h, 2)
    mate = a * 2 + 1 - b
    twin = xh * 2 + 1 - c
    tokens = xf_ref.shape[0]
    depth = w_ref.shape[0]
    width = gain_ref.shape[1]
    half = width // 2
    feat = ob_ref.shape[1]

    def rows_of(source):
        return pl.ds(pl.multiple_of(source * depth, depth), depth)

    w_loads = [
        pltpu.make_async_copy(
            w_ref.at[:, pl.ds(p * width, width)], wbuf.at[p, rows_of(s)], load_sem.at[p]
        )
        for p in range(3)
    ]
    x_loads = [
        pltpu.make_async_copy(xf_ref, xbuf.at[pl.ds(0, tokens)], load_sem.at[3]),
        pltpu.make_async_copy(xb_ref, xbuf.at[pl.ds(tokens, tokens)], load_sem.at[4]),
    ]
    o_loads = [
        pltpu.make_async_copy(cot_ref, cot, load_sem.at[5]),
        pltpu.make_async_copy(init_ref, init, load_sem.at[6]),
        pltpu.make_async_copy(gain_ref, gain, load_sem.at[7]),
    ]
    for p in (1, 2, 0):
        w_loads[p].start()
    for load in x_loads + o_loads:
        load.start()

    barrier = pltpu.get_barrier_semaphore()

    def greet(seq_index, head_index):
        pl.semaphore_signal(barrier, inc=1, device_id=(seq_index, head_index), device_id_type=MESH)

    for e in range(1, chain):
        greet(lax.rem(a + e, chain) * 2 + b, h)
    greet(mate, h)
    for e in range(1, pairs):
        greet(s, lax.rem(xh + e, pairs) * 2 + c)
    greet(s, twin)
    pl.semaphore_wait(barrier, chain + pairs)

    UP, DOWN, CROSS = 0, 1, 2
    early = (2, 1)
    kv = ((1, 0), (1, 1), (2, 0), (2, 1))
    kv_crossing = ((1, 0), (1, 1), (2, 0))
    q_only = ((0, 0), (0, 1))
    sub = depth // 2

    def shard_copy(piece, sa, sb, way):
        p, r = piece
        source = sa * 2 + sb
        rows = pl.ds(pl.multiple_of(source * depth + r * sub, sub), sub)
        to = {UP: s + 2, DOWN: s - 2, CROSS: mate}[way]
        return pltpu.make_async_remote_copy(
            src_ref=wbuf.at[p, rows],
            dst_ref=wbuf.at[p, rows],
            send_sem=wsend.at[way, source, p, r],
            recv_sem=wrecv.at[source, p, r],
            device_id=(to, h),
            device_id_type=MESH,
        )

    def arrived(piece, sa, sb):
        shard_copy(piece, sa, sb, CROSS).wait_recv()

    def project(source, columns):
        x = xbuf[:, pl.ds(pl.multiple_of(source * depth, depth), depth)]
        for p in columns:
            acc[p] += dot(x, wbuf[p, rows_of(source)])

    def start_up(piece, sa, sb):
        @pl.when(a < chain - 1)
        def _():
            shard_copy(piece, sa, sb, UP).start()

    def start_down(piece, sa, sb):
        @pl.when(a > 0)
        def _():
            shard_copy(piece, sa, sb, DOWN).start()

    def pass_on(d, piece, sb, crosses):
        @pl.when(a - d >= 0)
        def _():
            arrived(piece, a - d, sb)
            start_up(piece, a - d, sb)
            if crosses:
                shard_copy(piece, a - d, sb, CROSS).start()

        @pl.when(a + d < chain)
        def _():
            arrived(piece, a + d, sb)
            start_down(piece, a + d, sb)
            if crosses:
                shard_copy(piece, a + d, sb, CROSS).start()

    def chain_products(d, columns):
        @pl.when(a - d >= 0)
        def _():
            project((a - d) * 2 + b, columns)

        @pl.when(a + d < chain)
        def _():
            project((a + d) * 2 + b, columns)

    def crossings(d, pieces, columns):
        def crossed(sa):
            for piece in pieces:
                arrived(piece, sa, 1 - b)
            project(sa * 2 + 1 - b, columns)

        @pl.when(a - d >= 0)
        def _():
            crossed(a - d)

        @pl.when((a + d < chain) & (d > 0))
        def _():
            crossed(a + d)

    for p in (1, 2):
        w_loads[p].wait()
        for r in range(2):
            start_up((p, r), a, b)
            start_down((p, r), a, b)
            shard_copy((p, r), a, b, CROSS).start()
    w_loads[0].wait()
    acc[...] = jnp.zeros_like(acc)
    for load in x_loads:
        load.wait()
    project(s, (1, 2))
    arrived(early, a, 1 - b)
    start_up(early, a, 1 - b)
    start_down(early, a, 1 - b)

    @pl.when(a == 0)
    def _():
        for piece in q_only:
            start_up(piece, a, b)

    @pl.when(a == chain - 1)
    def _():
        for piece in q_only:
            start_down(piece, a, b)

    def kv_lap(d, carry):
        for piece in kv:
            pass_on(d, piece, b, piece != early)
        pass_on(d, early, 1 - b, False)

        @pl.when(a - d == 0)
        def _():
            for piece in q_only:
                start_up(piece, a, b)

        @pl.when(a + d == chain - 1)
        def _():
            for piece in q_only:
                start_down(piece, a, b)

        chain_products(d, (1, 2))
        crossings(d - 1, kv_crossing, (1, 2))
        return carry

    lax.fori_loop(1, chain, kv_lap, 0)
    for piece in q_only:
        shard_copy(piece, a, b, CROSS).start()
    project(s, (0,))
    crossings(chain - 1, kv_crossing, (1, 2))

    my_half = pl.ds(pl.multiple_of(b * half, half), half)
    far_half = pl.ds(pl.multiple_of((1 - b) * half, half), half)

    def step1_copy(i):
        return pltpu.make_async_remote_copy(
            src_ref=st_own.at[i, far_half],
            dst_ref=st_peer.at[i],
            send_sem=st_ssem.at[i, 0],
            recv_sem=st_rsem.at[i, 0],
            device_id=(mate, h),
            device_id_type=MESH,
        )

    def step2_copy(i, to, slot):
        return pltpu.make_async_remote_copy(
            src_ref=st_tot.at[i],
            dst_ref=st_z.at[i, slot],
            send_sem=z_ssem.at[i, to],
            recv_sem=z_rsem.at[i, slot],
            device_id=(to * 2 + b, h),
            device_id_type=MESH,
        )

    def step3_copy(i):
        return pltpu.make_async_remote_copy(
            src_ref=st_half.at[i],
            dst_ref=st_far.at[i],
            send_sem=st_ssem.at[i, 1],
            recv_sem=st_rsem.at[i, 1],
            device_id=(mate, h),
            device_id_type=MESH,
        )

    def after(i, x, y):
        return (x < y) if i == 2 else (x > y)

    def later(i):
        return 0 if i == 2 else 1

    def step1(i, state):
        st_own[i] = state.astype(BF16)
        step1_copy(i).start()

    def step2(i):
        step1_copy(i).wait_recv()
        st_tot[i] = (st_own[i, my_half].astype(F32) + st_peer[i].astype(F32)).astype(BF16)
        for e in range(1, chain):
            for to in (a - e, a + e):

                @pl.when(after(i, to, a) & (to >= 0) & (to < chain))
                def _():
                    step2_copy(i, to, a).start()

    def step3(i):
        half32[...] = jnp.zeros_like(half32)
        for source in range(chain):

            @pl.when(after(i, a, source))
            def _():
                step2_copy(i, source, source).wait_recv()
                half32[...] += st_z[i, source].astype(F32)

        whole32[i, my_half] = half32[...]

        @pl.when(b == later(i))
        def _():
            st_half[i] = half32[...].astype(BF16)
            whole32[i, my_half] += st_peer[i].astype(F32)

        @pl.when(b != later(i))
        def _():
            st_half[i] = (half32[...] + st_own[i, my_half].astype(F32)).astype(BF16)

        step3_copy(i).start()

    def step4(i):
        step3_copy(i).wait_recv()
        whole32[i, far_half] = st_far[i].astype(F32)
        return whole32[i]

    def part(p, mb):
        return acc[p, pl.ds(mb * tokens, tokens)].astype(BF16)

    kb, vb = part(1, 1), part(2, 1)
    step1(0, t_dot(kb, vb))
    step1(1, t_dot(part(1, 0), part(2, 0)))

    def q_lap(d, carry):
        for piece in q_only:
            pass_on(d, piece, b, True)
        chain_products(d, (0,))
        crossings(d - 1, q_only, (0,))
        return carry

    lax.fori_loop(1, 2, q_lap, 0)
    step2(0)
    step2(1)
    lax.fori_loop(2, chain, q_lap, 0)
    step3(0)
    step3(1)
    crossings(chain - 1, q_only, (0,))

    for load in o_loads:
        load.wait()
    positions = lax.broadcasted_iota(jnp.int32, (tokens, tokens), 0)
    others = lax.broadcasted_iota(jnp.int32, (tokens, tokens), 1)
    causal = others <= positions

    def masked(scores):
        return jnp.where(causal, scores, 0.0).astype(BF16)

    gains = gain[...]
    kb, vb, qb = part(1, 1), part(2, 1), part(0, 1)
    scores = masked(dot_t(qb, kb))
    prefix = (step4(0) + init[1, 0]).astype(BF16)
    output = dot(qb, prefix) + dot(scores, vb)
    scale = lax.rsqrt(jnp.mean(output * output, -1, keepdims=True) + epsilon)
    weighted = cot[...] * gains
    d_out = scale * weighted - output * (
        scale * scale * scale * jnp.mean(output * weighted, -1, keepdims=True)
    )
    d_out = d_out.astype(BF16)
    step1(2, t_dot(qb, d_out))
    d_scores = masked(dot_t(d_out, vb))
    dq = (dot_t(d_out, prefix) + dot(d_scores, kb)).astype(BF16)
    step2(2)
    dk_near = t_dot(d_scores, qb)
    dv_near = t_dot(scores, d_out)

    kf, vf, qf = part(1, 0), part(2, 0), part(0, 0)
    prefix_f = (step4(1) + init[0, 0]).astype(BF16)
    out_f = dot(qf, prefix_f) + dot(masked(dot_t(qf, kf)), vf)
    scale_f = lax.rsqrt(jnp.mean(out_f * out_f, -1, keepdims=True) + epsilon)
    of_ref[...] = out_f * scale_f * gains

    step3(2)
    suffix = step4(2).astype(BF16)
    dk = (dot_t(vb, suffix) + dk_near).astype(BF16)
    dv = (dot(kb, suffix) + dv_near).astype(BF16)

    part_rows = tokens // 2
    grads = [[g[k * part_rows : (k + 1) * part_rows] for g in (dq, dk, dv)] for k in range(2)]

    def product(j, k):
        rows = pl.ds(pl.multiple_of(j * feat, feat), feat)
        return sum(dot_t(grads[k][p], wbuf[p, rows]) for p in range(3))

    def twin_copy(slot, k):
        return pltpu.make_async_remote_copy(
            src_ref=c_send.at[slot, k],
            dst_ref=c_recv.at[slot, k],
            send_sem=c_ssem.at[slot, k],
            recv_sem=c_rsem.at[slot, k],
            device_id=(s, twin),
            device_id_type=MESH,
        )

    def pair_copy(to, slot, k):
        return pltpu.make_async_remote_copy(
            src_ref=x_send.at[to, k],
            dst_ref=x_recv.at[slot, k],
            send_sem=x_ssem.at[to, k],
            recv_sem=x_rsem.at[slot, k],
            device_id=(s, to * 2 + c),
            device_id_type=MESH,
        )

    def for_twin(to):
        for k in range(2):
            c_send[to, k] = product(to * 2 + 1 - c, k).astype(BF16)
            twin_copy(to, k).start()

    def twin_sum(to, k):
        mine = product(to * 2 + c, k)
        twin_copy(to, k).wait_recv()
        return mine + c_recv[to, k].astype(F32)

    def pair_lap(e, carry):
        to = lax.rem(xh + e, pairs)
        for_twin(to)
        for k in range(2):
            x_send[to, k] = twin_sum(to, k).astype(BF16)
            pair_copy(to, xh, k).start()
        return carry

    lax.fori_loop(1, pairs, pair_lap, 0)
    for_twin(xh)
    totals = [twin_sum(xh, k) for k in range(2)]
    for k in range(2):
        total = totals[k]
        for e in range(1, pairs):
            source = lax.rem(xh + e, pairs)
            pair_copy(source, source, k).wait_recv()
            total += x_recv[source, k].astype(F32)
        ob_ref[pl.ds(k * part_rows, part_rows)] = total.astype(BF16)

    def drain_chain(sa, carry):
        def left_chain(piece, sb):
            @pl.when((sa <= a) & (a < chain - 1))
            def _():
                shard_copy(piece, sa, sb, UP).wait_send()

            @pl.when((sa >= a) & (a > 0))
            def _():
                shard_copy(piece, sa, sb, DOWN).wait_send()

        for piece in kv + q_only:
            left_chain(piece, b)
        left_chain(early, 1 - b)
        for piece in kv_crossing + q_only:
            shard_copy(piece, sa, b, CROSS).wait_send()
        for i in range(3):

            @pl.when(after(i, sa, a))
            def _():
                step2_copy(i, sa, a).wait_send()

        return carry

    lax.fori_loop(0, chain, drain_chain, 0)
    shard_copy(early, a, b, CROSS).wait_send()
    for i in range(3):
        step1_copy(i).wait_send()
        step3_copy(i).wait_send()
    for k in range(2):
        for slot in range(pairs):
            twin_copy(slot, k).wait_send()
        for e in range(1, pairs):
            pair_copy(lax.rem(xh + e, pairs), xh, k).wait_send()


def body(n, hn, fwd_tokens, bwd_tokens, qkv_weight, head_gain, out_cotangent, initial_state):
    tokens, model = fwd_tokens.shape
    width = head_gain.shape[0]
    feat = model // hn
    chain, pairs = n // 2, hn // 2
    hbm = pl.BlockSpec(memory_space=pltpu.HBM)
    vmem = pl.BlockSpec(memory_space=pltpu.VMEM)
    dma = pltpu.SemaphoreType.DMA
    return pl.pallas_call(
        functools.partial(kernel, n, hn),
        out_shape=(
            jax.ShapeDtypeStruct((tokens, width), F32),
            jax.ShapeDtypeStruct((tokens, feat), BF16),
        ),
        in_specs=[hbm] * 6,
        out_specs=(vmem, vmem),
        scratch_shapes=[
            pltpu.VMEM((2 * tokens, model), BF16),
            pltpu.VMEM((3, model, width), BF16),
            pltpu.VMEM((3, 2 * tokens, width), F32),
            pltpu.VMEM((tokens, width), F32),
            pltpu.VMEM((2, 1, width, width), F32),
            pltpu.VMEM((1, width), F32),
            pltpu.VMEM((3, width, width), BF16),
            pltpu.VMEM((3, width // 2, width), BF16),
            pltpu.VMEM((3, width // 2, width), BF16),
            pltpu.VMEM((3, chain, width // 2, width), BF16),
            pltpu.VMEM((3, width // 2, width), BF16),
            pltpu.VMEM((3, width // 2, width), BF16),
            pltpu.VMEM((width // 2, width), F32),
            pltpu.VMEM((3, width, width), F32),
            pltpu.VMEM((pairs, 2, tokens // 2, feat), BF16),
            pltpu.VMEM((pairs, 2, tokens // 2, feat), BF16),
            pltpu.VMEM((pairs, 2, tokens // 2, feat), BF16),
            pltpu.VMEM((pairs, 2, tokens // 2, feat), BF16),
            dma((8,)),
            dma((3, n, 3, 2)),
            dma((n, 3, 2)),
            dma((3, 2)),
            dma((3, 2)),
            dma((3, chain)),
            dma((3, chain)),
            dma((pairs, 2)),
            dma((pairs, 2)),
            dma((pairs, 2)),
            dma((pairs, 2)),
        ],
        compiler_params=pltpu.CompilerParams(
            collective_id=0, has_side_effects=True, vmem_limit_bytes=63 * 1024 * 1024 + 512 * 1024
        ),
    )(fwd_tokens, bwd_tokens, qkv_weight, head_gain.reshape(1, width), out_cotangent, initial_state)


def solution(mesh):
    return jax.shard_map(
        functools.partial(body, mesh.shape["seq"], mesh.shape["heads"]),
        mesh=mesh,
        in_specs=(
            P("seq", None),
            P("seq", None),
            P("seq", "heads"),
            P("heads"),
            P("seq", "heads"),
            P(None, "heads", None, None),
        ),
        out_specs=(P("seq", "heads"), P("seq", "heads")),
        check_vma=False,
    )
```

time: 125 us -> 117 us (0.936)
  Pallas kernels: 117 us -> 113 us
  local copies, waits for them, and re-layouts: 6.88 us -> 3.54 us
    pallas_call x1, Pallas kernels: 117 us -> 113 us  [body(): pl.pallas_call(functools.partial(kernel, n, hn), out_shape=(jax.ShapeDtyp...]
    unnamed x12 -> x2, local copies, waits for them, and re-layouts: 6.88 us -> 3.54 us
where the time goes in v2:
time: 117 us
  Pallas kernels  113 us (97%)
  local copies, waits for them, and re-layouts  3.54 us (3%)
    pallas_call x1, Pallas kernels, body(): pl.pallas_call(functools.partial(kernel, n, hn), out_shape=(jax.ShapeDtyp...  113 us
    unnamed x2, local copies, waits for them, and re-layouts  3.54 us

profile of v2, /device:TPU:0, one launch (start us, length us, event | category | flops | bytes accessed | tf_op | source)
XLA Modules:
  0.0 117.0 jit_solution(5946841858648132367)
XLA Ops:
  0.6 112.8 %shard_map.77 = (f32[256,256]{1,0:T(8,128)}, bf16[256,1024]{1,0:T(8,128)(2,1)}) custom-call(bf16[256,4096]{1,0:T(8,128)(2,1)} %xf_ref.1, bf16[256,4096]{1,0:T(8,128)(2,1)} %xb_ref.1, bf16[512,768]{1,0:T(8,128)(2,1)} %w_ref.1, f32[1,256]{1,0:T(1,128)} %bitcast.1, f32[256,256]{1,0:T(8,128)} %cot_ref.1, f32[2,1,256,256]{3,2,1,0:T(8,128)} %init_ref.1), custom_call_target="tpu_custom_call" | custom-call | tf_op jit(solution)/shard_map/pallas_call | solution.py:483
  113.4 1.7 %copy.10 = f32[256,256]{1,0:T(8,128)} copy(f32[256,256]{1,0:T(8,128)} %get-tuple-element.4) | data formatting | bytes 524288
  115.1 1.9 %copy.11 = bf16[256,1024]{1,0:T(8,128)(2,1)} copy(bf16[256,1024]{1,0:T(8,128)(2,1)} %get-tuple-element.5) | data formatting | bytes 1048576

commit v3 on v2

--- a/solution.py
+++ b/solution.py
@@ -231,13 +231,16 @@
             for piece in q_only:
                 start_down(piece, a, b)
 
+        @pl.when(d == 1)
+        def _():
+            for piece in q_only:
+                shard_copy(piece, a, b, CROSS).start()
+
         chain_products(d, (1, 2))
         crossings(d - 1, kv_crossing, (1, 2))
         return carry
 
     lax.fori_loop(1, chain, kv_lap, 0)
-    for piece in q_only:
-        shard_copy(piece, a, b, CROSS).start()
     project(s, (0,))
     crossings(chain - 1, kv_crossing, (1, 2))
 
@@ -326,7 +329,6 @@
 
     kb, vb = part(1, 1), part(2, 1)
     step1(0, t_dot(kb, vb))
-    step1(1, t_dot(part(1, 0), part(2, 0)))
 
     def q_lap(d, carry):
         for piece in q_only:
@@ -337,10 +339,8 @@
 
     lax.fori_loop(1, 2, q_lap, 0)
     step2(0)
-    step2(1)
     lax.fori_loop(2, chain, q_lap, 0)
     step3(0)
-    step3(1)
     crossings(chain - 1, q_only, (0,))
 
     for load in o_loads:
@@ -370,16 +370,12 @@
     dk_near = t_dot(d_scores, qb)
     dv_near = t_dot(scores, d_out)
 
-    kf, vf, qf = part(1, 0), part(2, 0), part(0, 0)
-    prefix_f = (step4(1) + init[0, 0]).astype(BF16)
-    out_f = dot(qf, prefix_f) + dot(masked(dot_t(qf, kf)), vf)
-    scale_f = lax.rsqrt(jnp.mean(out_f * out_f, -1, keepdims=True) + epsilon)
-    of_ref[...] = out_f * scale_f * gains
-
+    step1(1, t_dot(part(1, 0), part(2, 0)))
     step3(2)
     suffix = step4(2).astype(BF16)
     dk = (dot_t(vb, suffix) + dk_near).astype(BF16)
     dv = (dot(kb, suffix) + dv_near).astype(BF16)
+    step2(1)
 
     part_rows = tokens // 2
     grads = [[g[k * part_rows : (k + 1) * part_rows] for g in (dq, dk, dv)] for k in range(2)]
@@ -429,6 +425,13 @@
     lax.fori_loop(1, pairs, pair_lap, 0)
     for_twin(xh)
     totals = [twin_sum(xh, k) for k in range(2)]
+    step3(1)
+    kf, vf, qf = part(1, 0), part(2, 0), part(0, 0)
+    prefix_f = (step4(1) + init[0, 0]).astype(BF16)
+    out_f = dot(qf, prefix_f) + dot(masked(dot_t(qf, kf)), vf)
+    scale_f = lax.rsqrt(jnp.mean(out_f * out_f, -1, keepdims=True) + epsilon)
+    of_ref[...] = out_f * scale_f * gains
+
     for k in range(2):
         total = totals[k]
         for e in range(1, pairs):

time: 117 us -> 113 us (0.966)
  Pallas kernels: 113 us -> 108 us
    pallas_call x1, Pallas kernels: 113 us -> 108 us  [body(): pl.pallas_call(functools.partial(kernel, n, hn), out_shape=(jax.ShapeDtyp...]
where the time goes in v3:
time: 113 us; the launch traced here: 112 us
  Pallas kernels  108 us (96%)
  local copies, waits for them, and re-layouts  3.54 us (3%)
    pallas_call x1, Pallas kernels, body(): pl.pallas_call(functools.partial(kernel, n, hn), out_shape=(jax.ShapeDtyp...  108 us
    unnamed x2, local copies, waits for them, and re-layouts  3.54 us

profile of v3, /device:TPU:0, one launch (start us, length us, event | category | flops | bytes accessed | tf_op | source)
XLA Modules:
  0.0 112.5 jit_solution(17630775606734058187)
XLA Ops:
  0.6 108.3 %shard_map.77 = (f32[256,256]{1,0:T(8,128)}, bf16[256,1024]{1,0:T(8,128)(2,1)}) custom-call(bf16[256,4096]{1,0:T(8,128)(2,1)} %xf_ref.1, bf16[256,4096]{1,0:T(8,128)(2,1)} %xb_ref.1, bf16[512,768]{1,0:T(8,128)(2,1)} %w_ref.1, f32[1,256]{1,0:T(1,128)} %bitcast.1, f32[256,256]{1,0:T(8,128)} %cot_ref.1, f32[2,1,256,256]{3,2,1,0:T(8,128)} %init_ref.1), custom_call_target="tpu_custom_call" | custom-call | tf_op jit(solution)/shard_map/pallas_call | solution.py:486
  108.9 1.7 %copy.10 = f32[256,256]{1,0:T(8,128)} copy(f32[256,256]{1,0:T(8,128)} %get-tuple-element.4) | data formatting | bytes 524288
  110.6 1.9 %copy.11 = bf16[256,1024]{1,0:T(8,128)(2,1)} copy(bf16[256,1024]{1,0:T(8,128)(2,1)} %get-tuple-element.5) | data formatting | bytes 1048576
